TPU v7x, 32 devices: a whole 2x2x4 slice. The times are simulated.
32 devices in a mesh: pipe: 4 (over y, x), dp: 8 (over z, core).
Axes of the slice: x: 2, y: 2, z: 4, core: 2. Of those that a mesh axis runs over, the one named last changes fastest.
Arguments:
- new_input: bfloat16 [4, 1024, 8192], P('pipe', 'dp'), may hold values from -400 to 400
- new_gain: bfloat16 [4, 8192], P('pipe'), may hold values from 0.5 to 1.5
- queries: bfloat16 [4, 1024, 4096], P('pipe', 'dp'), may hold values from -5 to 5
- new_keys: bfloat16 [4, 1024, 512], P('pipe', 'dp'), may hold values from -5 to 5
- context_grad: bfloat16 [4, 1024, 4096], P('pipe', 'dp'), may hold values from -0.08984375 to 0.08984375
- segment_ids: int32 [4, 1024], P('pipe', 'dp'), may hold values from 0 to 15, never falling along the last dimension, each value on 1 to 128 neighbouring positions
- frozen_input: bfloat16 [4, 1024, 8192], P('pipe', 'dp'), may hold values from -400 to 400
- frozen_gain: bfloat16 [4, 8192], P('pipe'), may hold values from 0.5 to 1.5
- output_grad: bfloat16 [4, 1024, 8192], P('pipe', 'dp'), may hold values from -6 to 6
- kv_grad: bfloat16 [4, 1024, 1024], P('pipe', 'dp'), may hold values from -18 to 18
- kv_weight: bfloat16 [4, 8192, 1024], P('pipe', 'dp'), may hold values from -0.0625 to 0.0625
Outputs:
- cot_below: bfloat16 [4, 1024, 8192], P('pipe', 'dp')
- value_grad: float32 [4, 8192, 512], P('pipe', 'dp')
Inputs may be any that keep to these rules, and one draw needn't show every extreme that they name: `segment_ids`: within a section the numbers never fall; every number of 0 to 15 appears, on 1 to 128 positions in a row, one on exactly 128.
All inputs are finite; a program needn't handle non-finite values.
Results may differ from a plain program's by a relative error of at most 0.0056.
Values may be sent and summed in bfloat16 or wider, within the bound.
No kernel may reach another device: no remote copies, remote signals or barrier semaphores. Data moves between devices by JAX's collectives and lax.ppermute only.
A program may use at most 128 MiB of HBM per device.

v0:
```python
import math

import jax
import jax.numpy as jnp
from jax import lax
from jax.sharding import PartitionSpec as P

HEAD = 128


norm_eps = 1e-05
masked_value = -1e30


def from_behind(array, axis, by):
    length = lax.axis_size(axis)
    pairs = [(i, i + by) for i in range(length) if 0 <= i + by < length]
    return lax.ppermute(array, axis, pairs)


def normalize(rows, gain):
    values = rows.astype(jnp.float32)
    inverse = lax.rsqrt(jnp.mean(values * values, axis=-1, keepdims=True) + norm_eps)
    return values * inverse * gain.astype(jnp.float32)


def norm_backward(rows, gain, upstream):
    values = rows.astype(jnp.float32)
    inverse = lax.rsqrt(jnp.mean(values * values, axis=-1, keepdims=True) + norm_eps)
    scaled = gain.astype(jnp.float32) * upstream
    inner_mean = jnp.mean(values * scaled, axis=-1, keepdims=True)
    return inverse * scaled - values * inverse * inverse * inverse * inner_mean


def masked_softmax(scores, visible):
    masked = jnp.where(visible, scores, masked_value)
    highest = jnp.max(masked, axis=-1, keepdims=True)
    weights = jnp.where(visible, jnp.exp(masked - highest), 0.0)
    return weights / jnp.sum(weights, axis=-1, keepdims=True)


def shards(
    new_input,
    new_gain,
    queries,
    new_keys,
    context_grad,
    segment_ids,
    frozen_input,
    frozen_gain,
    output_grad,
    kv_grad,
    kv_weight,
):
    tok_rows = queries.shape[1]
    kv_width = new_keys.shape[2]
    kv_heads = kv_width // HEAD
    group_size = queries.shape[2] // kv_width
    seg_rows = segment_ids[0]
    position = jnp.arange(tok_rows, dtype=jnp.int32)
    visible = (seg_rows[:, None] == seg_rows[None, :]) & (position[None, :] <= position[:, None])
    query_four = queries[0].reshape(tok_rows, kv_heads, group_size, HEAD)
    grad_four = context_grad[0].reshape(tok_rows, kv_heads, group_size, HEAD)
    key_three = new_keys[0].reshape(tok_rows, kv_heads, HEAD)
    scores = jnp.einsum(
        "tkgd,jkd->kgtj", query_four, key_three, preferred_element_type=jnp.float32
    ) / math.sqrt(HEAD)
    attention = masked_softmax(scores, visible).astype(jnp.bfloat16)
    value_cot = (
        jnp.einsum("kgtj,tkgd->jkd", attention, grad_four, preferred_element_type=jnp.float32)
        .reshape(tok_rows, kv_width)
        .astype(jnp.bfloat16)
    )
    normed_new = normalize(new_input[0], new_gain[0]).astype(jnp.bfloat16)
    columns = lax.all_to_all(normed_new, "dp", split_axis=1, concat_axis=0, tiled=True)
    value_grad = lax.dot_general(
        columns,
        lax.all_gather(value_cot, "dp", axis=0, tiled=True),
        (((0,), (0,)), ((), ())),
        preferred_element_type=jnp.float32,
    )
    frozen_cot = kv_grad[0]
    weight_rows = kv_weight[0]
    column_cot = lax.dot_general(
        lax.all_gather(frozen_cot, "dp", axis=0, tiled=True),
        weight_rows,
        (((1,), (1,)), ((), ())),
        preferred_element_type=jnp.float32,
    ).astype(jnp.bfloat16)
    normed_cot = lax.all_to_all(column_cot, "dp", split_axis=0, concat_axis=1, tiled=True)
    normed_cot = lax.optimization_barrier(normed_cot)
    input_cot = output_grad[0].astype(jnp.float32) + norm_backward(
        frozen_input[0], frozen_gain[0], normed_cot.astype(jnp.float32)
    )
    cot_below = from_behind(input_cot.astype(jnp.bfloat16), "pipe", -1)
    return (cot_below[None], value_grad[None])


def solution(mesh):
    placed = (
        P("pipe", "dp", None),
        P("pipe", None),
        P("pipe", "dp", None),
        P("pipe", "dp", None),
        P("pipe", "dp", None),
        P("pipe", "dp"),
        P("pipe", "dp", None),
        P("pipe", None),
        P("pipe", "dp", None),
        P("pipe", "dp", None),
        P("pipe", "dp", None),
    )
    return jax.shard_map(
        shards,
        mesh=mesh,
        in_specs=placed,
        out_specs=(P("pipe", "dp", None), P("pipe", "dp", None)),
        check_vma=False,
    )
```

profile of v0, /device:TPU:10, one launch (start us, length us, event | category | flops | bytes accessed | tf_op | source)
XLA Modules:
  0.0 179.5 jit_solution(7565307618095948066)
XLA Ops:
  7.2 0.0 copy-start
  7.2 0.0 all-gather.6.cloned.1.call-start
  7.2 0.7 all-gather.6.cloned.1.call-update
  7.9 32.0 %all-gather.6.cloned.1.call-done = bf16[1,1024,1024]{2,1,0:T(8,128)(2,1)} async-done(((bf16[1,128,1024]{2,1,0:T(8,128)(2,1)}), bf16[1,1024,1024]{2,1,0:T(8,128)(2,1)}) %all-gather.6.cloned.1.call-update) | async-done | bytes 2097168 | tf_op jit(solution)/shard_map/all_gather | solution.py:85
  39.9 0.0 copy-done
  39.9 5.3 %fusion.12 = bf16[1024,1024]{1,0:T(8,128)(2,1)} fusion(bf16[1,1024,1024]{2,1,0:T(8,128)(2,1)S(1)} %copy-done, bf16[1,1024,1024]{2,1,0:T(8,128)(2,1)} %all-gather.6.cloned.1.call-done), kind=kOutput, calls=%fused_computation.21 | convolution fusion | flops 2148532224 | bytes 6291456 | tf_op jit(solution)/shard_map/dot_general | solution.py:84
  45.2 0.0 copy-start.5
  45.2 0.0 copy-start.4
  45.2 4.9 %all-to-all-start = ((bf16[8,128,1024]{2,1,0:T(8,128)(2,1)}), bf16[8,128,1024]{2,1,0:T(8,128)(2,1)}, u32[]{:S(2)}, u32[]{:S(2)}) async-start(bf16[8,128,1024]{2,1,0:T(8,128)(2,1)} %bitcast.58), calls=%async_computation | async-start | bytes 4194304 | tf_op jit(solution)/shard_map/all_to_all | solution.py:90
  50.1 0.0 all-gather.4.cloned.1.call-start
  50.1 0.0 copy-done.5
  50.1 0.0 copy-done.4
  50.1 0.0 copy-start.8
  50.1 1.2 copy.37
  51.4 1.6 copy.35
  53.0 0.0 copy-done.8
  53.0 0.1 fusion.33
  53.1 3.6 %fusion.40 = (f32[4,8,128]{2,1,0:T(8,128)S(1)}, f32[4,8,128,128]{2,3,1,0:T(8,128)}) fusion(pred[128,128]{0,1:T(8,128)(4,1)S(1)} %fusion.33, bf16[128,4,8,128]{3,2,1,0:T(8,128)(2,1)} %bitcast.62, bf16[128,4,128,1]{2,1,0,3:T(4,128)(2,1)S(1)} %bitcast.66), kind=kOutput, calls=%fused_computation.40 | convolution fusion | flops 136839296 | bytes 3309568 | tf_op jit(solution)/shard_map/sub | solution.py:38
  56.7 0.0 copy-start.6
  56.7 0.0 copy-start.7
  56.7 2.7 %fusion.18 = bf16[4,128,128]{1,2,0:T(8,128)(2,1)} fusion(bf16[128,4,8,128]{0,3,2,1:T(8,128)(2,1)S(1)} %bitcast.61, f32[4,8,128,128]{2,3,1,0:T(8,128)} %get-tuple-element.5, f32[4,8,128]{2,1,0:T(8,128)S(1)} %get-tuple-element.4), kind=kOutput, calls=%fused_computation.25 | convolution fusion | flops 135331840 | bytes 3293184 | tf_op jit(solution)/shard_map/kgtj,tkgd->jkd/dot_general | solution.py:70
  59.4 0.0 all-gather.4.cloned.1.call-update
  59.4 0.0 copy-done.6
  59.4 0.1 convert_reduce_fusion
  59.5 0.0 copy-done.7
  59.6 4.1 %copy.24 = bf16[1,128,8192]{1,2,0:T(8,128)(2,1)} copy(bf16[1,128,8192]{2,1,0:T(8,128)(2,1)} %param.11) | data formatting | bytes 4194304 | tf_op args[0]
  63.6 0.0 copy-start.1
  63.6 2.8 %multiply_reduce_fusion = f32[128]{0:T(128)S(1)} fusion(bf16[1,128,8192]{1,2,0:T(8,128)(2,1)} %copy.24), kind=kLoop, calls=%fused_computation.13 | loop fusion | flops 3145600 | bytes 2097664 | tf_op jit(solution)/shard_map/reduce_sum | solution.py:23
  66.5 0.0 copy-done.1
  66.5 2.7 %multiply_convert_fusion = bf16[128,8,1024]{0,2,1:T(8,128)(2,1)} fusion(f32[8,1024]{1,0:T(8,128)S(1)} %reshape.59, f32[128]{0:T(128)S(1)} %add_rsqrt_fusion, bf16[128,8,1024]{0,2,1:T(8,128)(2,1)S(1)} %bitcast.57), kind=kLoop, calls=%fused_computation.12 | loop fusion | flops 4194304 | bytes 4227584 | tf_op jit(solution)/shard_map/convert_element_type | solution.py:74
  69.2 34.9 %all-to-all-done = bf16[8,128,1024]{2,1,0:T(8,128)(2,1)} async-done(((bf16[8,128,1024]{2,1,0:T(8,128)(2,1)}), bf16[8,128,1024]{2,1,0:T(8,128)(2,1)}, u32[]{:S(2)}, u32[]{:S(2)}) %all-to-all-start) | async-done | bytes 2097184 | tf_op jit(solution)/shard_map/all_to_all | solution.py:90
  104.1 7.8 %all-to-all-start.1 = ((bf16[128,8,1024]{0,2,1:T(8,128)(2,1)}), bf16[128,8,1024]{0,2,1:T(8,128)(2,1)}, u32[]{:S(2)}, u32[]{:S(2)}) async-start(bf16[128,8,1024]{0,2,1:T(8,128)(2,1)} %multiply_convert_fusion), calls=%async_computation.1 | async-start | bytes 4194304 | tf_op jit(solution)/shard_map/all_to_all | solution.py:75
  111.9 0.0 copy-start.2
  111.9 1.9 %copy.36 = bf16[8,16,8,1024]{3,2,0,1:T(8,128)(2,1)S(1)} copy(bf16[8,16,8,1024]{3,2,1,0:T(8,128)(2,1)} %bitcast.23) | data formatting | bytes 4194304 | tf_op jit(solution)/shard_map/all_to_all | solution.py:90
  113.9 0.3 copy-done.2
  114.1 0.0 copy-start.3
  114.2 1.2 fusion.1
  115.4 0.3 copy-done.3
  115.7 3.1 %fusion.7 = bf16[128,8192]{1,0:T(8,128)(2,1)} fusion(bf16[128,8192]{1,0:T(8,128)(2,1)S(1)} %bitcast.56, bf16[1,128,8192]{2,1,0:T(8,128)(2,1)S(1)} %copy-done.3, bf16[1,128,8192]{2,1,0:T(8,128)(2,1)S(1)} %copy-done.2, f32[128]{0:T(128)S(1)} %get-tuple-element.7, f32[8192]{0:T(1024)S(1)} %bitcast.64, f32[128]{0:T(128)S(1)} %get-tuple-element.6), kind=kLoop, calls=%fused_computation.10 | loop fusion | flops 12582912 | bytes 8422400 | tf_op jit(solution)/shard_map/convert_element_type | solution.py:95
  118.8 2.5 %collective-permute-start = (bf16[128,8192]{1,0:T(8,128)(2,1)}, bf16[128,8192]{1,0:T(8,128)(2,1)}, u32[]{:S(2)}, u32[]{:S(2)}) collective-permute-start(bf16[128,8192]{1,0:T(8,128)(2,1)} %fusion.7), channel_id=1, source_target_pairs={{8,0},{16,8},{24,16},{9,1},{17,9},{25,17},{10,2},{18,10},{26,18},{... | collective-permute-start | bytes 6291464 | tf_op jit(solution)/shard_map/ppermute | solution.py:18
  121.3 36.2 %all-to-all-done.1 = bf16[128,8,1024]{0,2,1:T(8,128)(2,1)} async-done(((bf16[128,8,1024]{0,2,1:T(8,128)(2,1)}), bf16[128,8,1024]{0,2,1:T(8,128)(2,1)}, u32[]{:S(2)}, u32[]{:S(2)}) %all-to-all-start.1) | async-done | bytes 2097184 | tf_op jit(solution)/shard_map/all_to_all | solution.py:75
  157.5 3.9 %copy.25 = bf16[8,128,1024]{2,1,0:T(8,128)(2,1)} copy(bf16[8,128,1024]{1,2,0:T(8,128)(2,1)} %bitcast.10) | data formatting | bytes 4194304 | tf_op jit(solution)/shard_map/all_to_all | solution.py:75
  161.4 0.0 all-gather.4.cloned.1.call-done
  161.4 4.5 %convolution_bitcast_fusion = f32[1,1024,512]{2,1,0:T(8,128)} fusion(bf16[1024,1024]{1,0:T(8,128)(2,1)} %bitcast.59, bf16[1024,512]{0,1:T(8,128)(2,1)} %all-gather.4.cloned.1.call-done), kind=kOutput, calls=%fused_computation.23 | convolution fusion | flops 1073741824 | bytes 5242880 | tf_op jit(solution)/shard_map/dot_general | solution.py:76
  165.9 3.7 %collective-permute-done = bf16[128,8192]{1,0:T(8,128)(2,1)} collective-permute-done((bf16[128,8192]{1,0:T(8,128)(2,1)}, bf16[128,8192]{1,0:T(8,128)(2,1)}, u32[]{:S(2)}, u32[]{:S(2)}) %collective-permute-start) | collective-permute-done | bytes 2097184 | tf_op jit(solution)/shard_map/ppermute | solution.py:18
  169.6 3.1 %copy.59 = bf16[1,128,8192]{2,1,0:T(8,128)(2,1)} copy(bf16[1,128,8192]{2,1,0:T(8,128)(2,1)} %bitcast.8) | data formatting | bytes 4194304
  (5 shorter events, 0.1 us)
Async XLA Ops:
  7.2 32.7 %copy-start = (bf16[1,1024,1024]{2,1,0:T(8,128)(2,1)S(1)}, bf16[1,1024,1024]{2,1,0:T(8,128)(2,1)}, u32[]{:S(2)}) copy-start(bf16[1,1024,1024]{2,1,0:T(8,128)(2,1)} %param.21) | copy-start | bytes 6291460
  7.2 32.7 %all-gather.6.cloned.1.call-start = ((), (), s32[]{:S(2)}) async-start(), calls=%async_computation.3 | async-start | bytes 2359296 | tf_op jit(solution)/shard_map/all_gather | solution.py:85
  45.2 4.9 %copy-start.5 = (bf16[1,128,512]{2,1,0:T(8,128)(2,1)S(1)}, bf16[1,128,512]{2,1,0:T(8,128)(2,1)}, u32[]{:S(2)}) copy-start(bf16[1,128,512]{2,1,0:T(8,128)(2,1)} %param.14) | copy-start | bytes 393220
  45.2 5.0 %copy-start.4 = (bf16[1,128,4096]{2,1,0:T(8,128)(2,1)S(1)}, bf16[1,128,4096]{2,1,0:T(8,128)(2,1)}, u32[]{:S(2)}) copy-start(bf16[1,128,4096]{2,1,0:T(8,128)(2,1)} %param.13) | copy-start | bytes 3145732
  45.2 58.9 %all-to-all-start = ((bf16[8,128,1024]{2,1,0:T(8,128)(2,1)}), bf16[8,128,1024]{2,1,0:T(8,128)(2,1)}, u32[]{:S(2)}, u32[]{:S(2)}) async-start(bf16[8,128,1024]{2,1,0:T(8,128)(2,1)} %bitcast.58), calls=%async_computation | async-start | bytes 4194304 | tf_op jit(solution)/shard_map/all_to_all | solution.py:90
  50.1 111.3 %all-gather.4.cloned.1.call-start = ((), (), s32[]{:S(2)}) async-start(), calls=%async_computation.2 | async-start | bytes 1179648 | tf_op jit(solution)/shard_map/all_gather | solution.py:78
  50.1 2.8 %copy-start.8 = (s32[1,128]{1,0:T(1,128)S(1)}, s32[1,128]{1,0:T(1,128)}, u32[]{:S(2)}) copy-start(s32[1,128]{1,0:T(1,128)} %param.16) | copy-start | bytes 1540
  56.7 2.7 %copy-start.6 = (bf16[1,8192]{1,0:T(2,128)(2,1)S(1)}, bf16[1,8192]{1,0:T(2,128)(2,1)}, u32[]{:S(2)}) copy-start(bf16[1,8192]{1,0:T(2,128)(2,1)} %param.12) | copy-start | bytes 49156
  56.7 2.8 %copy-start.7 = (bf16[1,8192]{1,0:T(2,128)(2,1)S(1)}, bf16[1,8192]{1,0:T(2,128)(2,1)}, u32[]{:S(2)}) copy-start(bf16[1,8192]{1,0:T(2,128)(2,1)} %param.18) | copy-start | bytes 49156
  63.6 2.8 %copy-start.1 = (bf16[1,128,8192]{1,2,0:T(8,128)(2,1)S(1)}, bf16[1,128,8192]{1,2,0:T(8,128)(2,1)}, u32[]{:S(2)}) copy-start(bf16[1,128,8192]{1,2,0:T(8,128)(2,1)} %copy.24) | copy-start | bytes 6291460
  104.1 53.4 %all-to-all-start.1 = ((bf16[128,8,1024]{0,2,1:T(8,128)(2,1)}), bf16[128,8,1024]{0,2,1:T(8,128)(2,1)}, u32[]{:S(2)}, u32[]{:S(2)}) async-start(bf16[128,8,1024]{0,2,1:T(8,128)(2,1)} %multiply_convert_fusion), calls=%async_computation.1 | async-start | bytes 4194304 | tf_op jit(solution)/shard_map/all_to_all | solution.py:75
  111.9 2.2 %copy-start.2 = (bf16[1,128,8192]{2,1,0:T(8,128)(2,1)S(1)}, bf16[1,128,8192]{2,1,0:T(8,128)(2,1)}, u32[]{:S(2)}) copy-start(bf16[1,128,8192]{2,1,0:T(8,128)(2,1)} %param.17) | copy-start | bytes 6291460
  114.1 1.6 copy-start.3
  118.8 50.8 %collective-permute-start = (bf16[128,8192]{1,0:T(8,128)(2,1)}, bf16[128,8192]{1,0:T(8,128)(2,1)}, u32[]{:S(2)}, u32[]{:S(2)}) collective-permute-start(bf16[128,8192]{1,0:T(8,128)(2,1)} %fusion.7), channel_id=1, source_target_pairs={{8,0},{16,8},{24,16},{9,1},{17,9},{25,17},{10,2},{18,10},{26,18},{... | collective-permute-start | bytes 6291464 | tf_op jit(solution)/shard_map/ppermute | solution.py:18
Sparse Core Ops, SparseCore 0:
  9.6 30.2 all-gather.5
  59.5 42.0 all-gather.3
where the time goes:
time: 181 us; the launch traced here: 180 us
  waiting for transfers between devices  107 us (59%)
  local copies, waits for them, and re-layouts  16.5 us (9%)
  matrix products  16.1 us (9%)
  starting transfers between devices  15.2 us (8%)
  between operations  14.1 us (8%)
  other arithmetic  10.1 us (6%)
    all_to_all x1, waiting for transfers between devices, shards(): lax.all_to_all(normed_new, 'dp', split_axis=1, concat_axis=0, tiled=True)  36.2 us
    all_to_all x1, waiting for transfers between devices, shards(): lax.all_to_all(column_cot, 'dp', split_axis=0, concat_axis=1, tiled=True)  34.9 us
    all_gather x1, waiting for transfers between devices, shards(): lax.all_gather(frozen_cot, 'dp', axis=0, tiled=True)  32 us
    unnamed x21, local copies, waits for them, and re-layouts  9.02 us
    all_to_all x1, starting transfers between devices, shards(): lax.all_to_all(normed_new, 'dp', split_axis=1, concat_axis=0, tiled=True)  7.84 us
    dot_general x1, matrix products, shards(): lax.dot_general(lax.all_gather(frozen_cot, 'dp', axis=0, tiled=True), wei...  5.28 us
    all_to_all x1, starting transfers between devices, shards(): lax.all_to_all(column_cot, 'dp', split_axis=0, concat_axis=1, tiled=True)  4.91 us
    dot_general x1, matrix products, shards(): lax.dot_general(columns, lax.all_gather(value_cot, 'dp', axis=0, tiled=Tr...  4.47 us
  transfers between devices with their start and end apart: 5, of which 4 were waited for; matrix products, arithmetic and copies ran while one was open for 19% of the time, Pallas kernels for 0%

commit v1 on v0

v1 whole, which is shorter than its diff:
```python
import functools
import math

import jax
import jax.numpy as jnp
from jax import lax
from jax.experimental import pallas as pl
from jax.experimental.pallas import tpu as pltpu
from jax.sharding import PartitionSpec as P

HEAD = 128
CHUNKS = 2


norm_eps = 1e-05
masked_value = -1e30
MIB = 1 << 20


def from_behind(array, axis, by):
    length = lax.axis_size(axis)
    pairs = [(i, i + by) for i in range(length) if 0 <= i + by < length]
    return lax.ppermute(array, axis, pairs)


def params(vmem):
    return pltpu.CompilerParams(vmem_limit_bytes=vmem * MIB)


def cost(flops, nbytes):
    return pl.CostEstimate(flops=flops, bytes_accessed=nbytes, transcendentals=0)


def norm_kernel(x_ref, gain_ref, out_ref):
    values = x_ref[...].astype(jnp.float32)
    inverse = lax.rsqrt(jnp.mean(values * values, axis=-1, keepdims=True) + norm_eps)
    parts, _, width = out_ref.shape
    for part in range(parts):
        cols = slice(part * width, (part + 1) * width)
        out_ref[part] = (
            values[:, cols] * inverse * gain_ref[:, cols].astype(jnp.float32)
        ).astype(out_ref.dtype)


def normalize(rows, gain, parts, chunk, chunks):
    tokens, width = rows.shape
    taken = tokens // chunks
    block = min(taken, 32)
    first = chunk * (taken // block)
    return pl.pallas_call(
        norm_kernel,
        grid=(taken // block,),
        in_specs=[
            pl.BlockSpec((block, width), lambda i: (first + i, 0)),
            pl.BlockSpec((1, width), lambda i: (0, 0)),
        ],
        out_specs=pl.BlockSpec((parts, block, width // parts), lambda i: (0, i, 0)),
        out_shape=jax.ShapeDtypeStruct((parts, taken, width // parts), jnp.bfloat16),
        compiler_params=params(16),
        cost_estimate=cost(4 * taken * width, 4 * taken * width),
        name="norm_forward",
    )(rows, gain)


def attend_kernel(query_ref, key_ref, grad_ref, row_seg_ref, col_seg_ref, out_ref):
    tokens = key_ref.shape[0]
    group = query_ref.shape[1] // HEAD
    at_query = lax.broadcasted_iota(jnp.int32, (tokens, tokens), 0)
    at_key = lax.broadcasted_iota(jnp.int32, (tokens, tokens), 1)
    visible = (col_seg_ref[...] == row_seg_ref[...]) & (at_key <= at_query)
    keys = key_ref[...]
    total = jnp.zeros((tokens, HEAD), jnp.float32)
    for head in range(group):
        cols = slice(head * HEAD, (head + 1) * HEAD)
        scores = lax.dot_general(
            query_ref[:, cols], keys, (((1,), (1,)), ((), ())),
            preferred_element_type=jnp.float32,
        ) / math.sqrt(HEAD)
        masked = jnp.where(visible, scores, masked_value)
        highest = jnp.max(masked, axis=-1, keepdims=True)
        weights = jnp.where(visible, jnp.exp(masked - highest), 0.0)
        attention = (weights / jnp.sum(weights, axis=-1, keepdims=True)).astype(jnp.bfloat16)
        total += lax.dot_general(
            attention, grad_ref[:, cols], (((0,), (0,)), ((), ())),
            preferred_element_type=jnp.float32,
        )
    out_ref[...] = total.astype(out_ref.dtype)


def attend(queries, keys, grads, segments):
    tokens, kv_width = keys.shape
    heads = kv_width // HEAD
    wide = queries.shape[1] // heads
    return pl.pallas_call(
        attend_kernel,
        grid=(heads,),
        in_specs=[
            pl.BlockSpec((tokens, wide), lambda i: (0, i)),
            pl.BlockSpec((tokens, HEAD), lambda i: (0, i)),
            pl.BlockSpec((tokens, wide), lambda i: (0, i)),
            pl.BlockSpec((1, tokens), lambda i: (0, 0)),
            pl.BlockSpec((tokens, 1), lambda i: (0, 0)),
        ],
        out_specs=pl.BlockSpec((tokens, HEAD), lambda i: (0, i)),
        out_shape=jax.ShapeDtypeStruct((tokens, kv_width), jnp.bfloat16),
        compiler_params=params(16),
        cost_estimate=cost(4 * tokens * tokens * queries.shape[1], 4 * tokens * queries.shape[1]),
        name="attend",
    )(queries, keys, grads, segments, segments.reshape(tokens, 1))


def project_kernel(rows_ref, weight_ref, out_ref):
    parts, taken, depth = rows_ref.shape
    out_ref[...] = lax.dot_general(
        rows_ref[...].reshape(parts * taken, depth), weight_ref[...], (((1,), (1,)), ((), ())),
        preferred_element_type=jnp.float32,
    ).astype(out_ref.dtype).reshape(out_ref.shape)


def project(rows, weight, chunk, chunks):
    parts, tokens, depth = rows.shape
    width = weight.shape[0]
    taken = tokens // chunks
    block = min(width, 256)
    return pl.pallas_call(
        project_kernel,
        grid=(width // block,),
        in_specs=[
            pl.BlockSpec((parts, taken, depth), lambda i: (0, chunk, 0)),
            pl.BlockSpec((block, depth), lambda i: (i, 0)),
        ],
        out_specs=pl.BlockSpec((parts, taken, block), lambda i: (0, 0, i)),
        out_shape=jax.ShapeDtypeStruct((parts, taken, width), jnp.bfloat16),
        compiler_params=params(48),
        cost_estimate=cost(2 * parts * taken * depth * width, 2 * (parts * taken * (depth + width) + width * depth)),
        name="project",
    )(rows, weight)


def backward_kernel(cot_ref, x_ref, gain_ref, grad_ref, out_ref):
    parts, _, width = cot_ref.shape
    values = x_ref[...].astype(jnp.float32)
    inverse = lax.rsqrt(jnp.mean(values * values, axis=-1, keepdims=True) + norm_eps)
    inner = jnp.zeros_like(inverse)
    for part in range(parts):
        cols = slice(part * width, (part + 1) * width)
        scaled = gain_ref[:, cols].astype(jnp.float32) * cot_ref[part].astype(jnp.float32)
        inner += jnp.sum(values[:, cols] * scaled, axis=-1, keepdims=True)
    factor = inverse * inverse * inverse * (inner / (parts * width))
    for part in range(parts):
        cols = slice(part * width, (part + 1) * width)
        scaled = gain_ref[:, cols].astype(jnp.float32) * cot_ref[part].astype(jnp.float32)
        out_ref[:, cols] = (
            grad_ref[:, cols].astype(jnp.float32) + inverse * scaled - values[:, cols] * factor
        ).astype(out_ref.dtype)


def norm_backward(cot, rows, gain, grads, chunk, chunks):
    parts, taken, part_width = cot.shape
    tokens, width = rows.shape
    block = min(taken, 32)
    first = chunk * (taken // block)
    return pl.pallas_call(
        backward_kernel,
        grid=(taken // block,),
        in_specs=[
            pl.BlockSpec((parts, block, part_width), lambda i: (0, i, 0)),
            pl.BlockSpec((block, width), lambda i: (first + i, 0)),
            pl.BlockSpec((1, width), lambda i: (0, 0)),
            pl.BlockSpec((block, width), lambda i: (first + i, 0)),
        ],
        out_specs=pl.BlockSpec((block, width), lambda i: (i, 0)),
        out_shape=jax.ShapeDtypeStruct((taken, width), jnp.bfloat16),
        compiler_params=params(24),
        cost_estimate=cost(10 * taken * width, 8 * taken * width),
        name="norm_backward",
    )(cot, rows, gain, grads)


def outer_kernel(columns_ref, cot_ref, *rest):
    out_ref = rest[-1]
    parts, taken, width = columns_ref.shape
    product = lax.dot_general(
        columns_ref[...].reshape(parts * taken, width),
        cot_ref[...].reshape(parts * taken, cot_ref.shape[2]),
        (((0,), (0,)), ((), ())),
        preferred_element_type=jnp.float32,
    )
    if len(rest) > 1:
        product += rest[0][...]
    out_ref[...] = product


def outer(columns, cot, before, chunk, chunks):
    parts, taken, width = columns.shape
    cot_width = cot.shape[2]
    block = min(width, 256)
    out_spec = pl.BlockSpec((block, cot_width), lambda i: (i, 0))
    operands = [columns, cot] + ([] if before is None else [before])
    return pl.pallas_call(
        outer_kernel,
        grid=(width // block,),
        in_specs=[
            pl.BlockSpec((parts, taken, block), lambda i: (0, 0, i)),
            pl.BlockSpec((parts, taken, cot_width), lambda i: (0, chunk, 0)),
        ] + ([] if before is None else [out_spec]),
        out_specs=out_spec,
        out_shape=jax.ShapeDtypeStruct((width, cot_width), jnp.float32),
        compiler_params=params(32),
        cost_estimate=cost(2 * parts * taken * width * cot_width, 4 * parts * taken * width),
        name="outer",
    )(*operands)


def exchange(blocks):
    return lax.all_to_all(blocks, "dp", split_axis=0, concat_axis=0, tiled=True)


def shards(
    new_input,
    new_gain,
    queries,
    new_keys,
    context_grad,
    segment_ids,
    frozen_input,
    frozen_gain,
    output_grad,
    kv_grad,
    kv_weight,
):
    parts = lax.axis_size("dp")
    chunks = CHUNKS
    kv_all = lax.all_gather(kv_grad[0], "dp", axis=0, tiled=False)
    columns = [exchange(normalize(new_input[0], new_gain, parts, 0, chunks))]
    value_cot = attend(queries[0], new_keys[0], context_grad[0], segment_ids)
    cot_all = lax.all_gather(value_cot, "dp", axis=0, tiled=False)
    below = []
    for chunk in range(chunks):
        own = exchange(project(kv_all, kv_weight[0], chunk, chunks))
        input_cot = norm_backward(own, frozen_input[0], frozen_gain, output_grad[0], chunk, chunks)
        below.append(from_behind(input_cot, "pipe", -1))
    for chunk in range(1, chunks):
        columns.append(exchange(normalize(new_input[0], new_gain, parts, chunk, chunks)))
    grad = None
    for chunk in range(chunks):
        grad = outer(columns[chunk], cot_all, grad, chunk, chunks)
    return (jnp.concatenate(below, axis=0)[None], grad[None])


def solution(mesh):
    placed = (
        P("pipe", "dp", None),
        P("pipe", None),
        P("pipe", "dp", None),
        P("pipe", "dp", None),
        P("pipe", "dp", None),
        P("pipe", "dp"),
        P("pipe", "dp", None),
        P("pipe", None),
        P("pipe", "dp", None),
        P("pipe", "dp", None),
        P("pipe", "dp", None),
    )
    return jax.shard_map(
        shards,
        mesh=mesh,
        in_specs=placed,
        out_specs=(P("pipe", "dp", None), P("pipe", "dp", None)),
        check_vma=False,
    )
```

time: 181 us -> 206 us (1.14)
  Pallas kernels: 0 us -> 25.5 us
  starting transfers between devices: 15.2 us -> 35.3 us
  matrix products: 16.1 us -> 0 us
  waiting for transfers between devices: 107 us -> 115 us
  other arithmetic: 10.1 us -> 3.05 us
  local copies, waits for them, and re-layouts: 16.5 us -> 11.3 us
    pallas_call x0 -> x9, Pallas kernels: none -> 25.5 us  [the longest x2 6.15 us: norm_backward(): pl.pallas_call(backward_kernel, grid=(taken // block,), in_specs=[pl.Bloc...]
    ppermute x1 -> x2, waiting for transfers between devices: 3.71 us -> 27 us  [from_behind(): return lax.ppermute(array, axis, pairs)]
    all_to_all x2 -> x4, waiting for transfers between devices: 71.1 us -> 49.2 us  [exchange(): return lax.all_to_all(blocks, 'dp', split_axis=0, concat_axis=0, tiled=True)]
    all_to_all x2 -> x4, starting transfers between devices: 12.8 us -> 30.9 us  [exchange(): return lax.all_to_all(blocks, 'dp', split_axis=0, concat_axis=0, tiled=True)]
    dot_general x3 -> x0, matrix products: 12.4 us -> none  [the longest x1 5.28 us: shards(): lax.dot_general(lax.all_gather(frozen_cot, 'dp', axis=0, tiled=True), wei...]
    all_gather x2, waiting for transfers between devices: 32 us -> 38.2 us  [the longest x1 38.2 us: shards(): kv_all = lax.all_gather(kv_grad[0], 'dp', axis=0, tiled=False)]
    all_to_all x2 -> x0, local copies, waits for them, and re-layouts: 5.84 us -> none  [the longest x1 3.9 us: shards(): lax.all_to_all(normed_new, 'dp', split_axis=1, concat_axis=0, tiled=True)]
    convert_element_type x2 -> x0, other arithmetic: 5.79 us -> none  [the longest x1 3.08 us: shards(): cot_below = from_behind(input_cot.astype(jnp.bfloat16), 'pipe', -1)]
  transfers between devices with their start and end apart: 5 -> 8, of which waited for: 4 -> 6; matrix products, arithmetic and copies ran while one was open for 19% -> 0% of each run, Pallas kernels for 0% -> 12%
where the time goes in v1:
time: 206 us; the launch traced here: 204 us
  waiting for transfers between devices  115 us (56%)
  starting transfers between devices  35.3 us (17%)
  Pallas kernels  25.5 us (12%)
  between operations  14.2 us (7%)
  local copies, waits for them, and re-layouts  11.3 us (5%)
  other arithmetic  3.05 us (1%)
    all_to_all x4, waiting for transfers between devices, exchange(): return lax.all_to_all(blocks, 'dp', split_axis=0, concat_axis=0, tiled=True)  49.2 us
    all_gather x1, waiting for transfers between devices, shards(): kv_all = lax.all_gather(kv_grad[0], 'dp', axis=0, tiled=False)  38.2 us
    all_to_all x4, starting transfers between devices, exchange(): return lax.all_to_all(blocks, 'dp', split_axis=0, concat_axis=0, tiled=True)  30.9 us
    ppermute x2, waiting for transfers between devices, from_behind(): return lax.ppermute(array, axis, pairs)  27 us
    unnamed x34, local copies, waits for them, and re-layouts  11.2 us
    pallas_call x2, Pallas kernels, norm_backward(): pl.pallas_call(backward_kernel, grid=(taken // block,), in_specs=[pl.Bloc...  6.15 us
    pallas_call x2, Pallas kernels, project(): pl.pallas_call(project_kernel, grid=(width // block,), in_specs=[pl.Block...  5.84 us
    pallas_call x2, Pallas kernels, outer(): pl.pallas_call(outer_kernel, grid=(width // block,), in_specs=[pl.BlockSp...  5.68 us
  transfers between devices with their start and end apart: 8, of which 6 were waited for; matrix products, arithmetic and copies ran while one was open for 0% of the time, Pallas kernels for 12%

profile of v1, /device:TPU:10, one launch (start us, length us, event | category | flops | bytes accessed | tf_op | source)
XLA Modules:
  0.0 204.3 jit_solution(6173775522579441891)
XLA Ops:
  7.2 0.0 all-gather.4.cloned.1.call-start
  7.2 0.7 all-gather.4.cloned.1.call-update
  7.9 0.0 copy-start.3
  7.9 1.6 copy-done.3
  9.5 0.8 copy-done.12
  10.3 1.3 norm_forward.3
  11.6 5.3 %all-to-all-start.3 = ((bf16[8,64,1024]{2,1,0:T(8,128)(2,1)}), bf16[8,64,1024]{2,1,0:T(8,128)(2,1)S(1)}, u32[]{:S(2)}, u32[]{:S(2)}) async-start(bf16[8,64,1024]{2,1,0:T(8,128)(2,1)} %norm_forward.3), calls=%async_computation.3 | async-start | bytes 2097152 | tf_op jit(solution)/shard_map/all_to_all | solution.py:216
  16.9 38.2 %all-gather.4.cloned.1.call-done.rows_ref = bf16[8,128,1024]{2,1,0:T(8,128)(2,1)} async-done(((bf16[1,128,1024]{2,1,0:T(8,128)(2,1)}), bf16[8,128,1024]{2,1,0:T(8,128)(2,1)}) %all-gather.4.cloned.1.call-update) | async-done | bytes 2097168 | tf_op jit(solution)/shard_map/all_gather | solution.py:234
  55.1 0.0 copy-done.5
  55.1 1.6 copy-done.6
  56.7 2.9 %project.2 = bf16[8,64,1024]{2,1,0:T(8,128)(2,1)} custom-call(bf16[8,128,1024]{2,1,0:T(8,128)(2,1)S(1)} %copy-done.6, bf16[1024,1024]{1,0:T(8,128)(2,1)S(1)} %bitcast.18), custom_call_target="tpu_custom_call" | custom-call | flops 1073741824 | bytes 4194304 | tf_op jit(solution)/shard_map/project/pallas_call | solution.py:125
  59.6 0.0 all-to-all-done.3.columns_ref
  59.6 9.1 %all-to-all-start = ((bf16[8,64,1024]{2,1,0:T(8,128)(2,1)}), bf16[8,64,1024]{2,1,0:T(8,128)(2,1)}, u32[]{:S(2)}, u32[]{:S(2)}) async-start(bf16[8,64,1024]{2,1,0:T(8,128)(2,1)} %project.2), calls=%async_computation | async-start | bytes 2097152 | tf_op jit(solution)/shard_map/all_to_all | solution.py:216
  68.8 1.6 copy-done.7
  70.4 2.9 %project.3 = bf16[8,64,1024]{2,1,0:T(8,128)(2,1)} custom-call(bf16[8,128,1024]{2,1,0:T(8,128)(2,1)S(1)} %copy-done.7, bf16[1024,1024]{1,0:T(8,128)(2,1)S(1)} %bitcast.19), custom_call_target="tpu_custom_call" | custom-call | flops 1073741824 | bytes 4194304 | tf_op jit(solution)/shard_map/project/pallas_call | solution.py:125
  73.3 18.6 %all-to-all-done.cot_ref = bf16[8,64,1024]{2,1,0:T(8,128)(2,1)} async-done(((bf16[8,64,1024]{2,1,0:T(8,128)(2,1)}), bf16[8,64,1024]{2,1,0:T(8,128)(2,1)}, u32[]{:S(2)}, u32[]{:S(2)}) %all-to-all-start) | async-done | bytes 1048608 | tf_op jit(solution)/shard_map/all_to_all | solution.py:216
  91.9 7.7 %all-to-all-start.1 = ((bf16[8,64,1024]{2,1,0:T(8,128)(2,1)}), bf16[8,64,1024]{2,1,0:T(8,128)(2,1)}, u32[]{:S(2)}, u32[]{:S(2)}) async-start(bf16[8,64,1024]{2,1,0:T(8,128)(2,1)} %project.3), calls=%async_computation.1 | async-start | bytes 2097152 | tf_op jit(solution)/shard_map/all_to_all | solution.py:216
  99.6 0.0 all-gather.6.cloned.1.call-start
  99.6 0.0 copy-done.16
  99.6 0.1 copy.14.col_seg_ref
  99.7 0.0 copy-done.15
  99.7 0.0 copy-done.10
  99.7 0.0 copy-done.11
  99.8 5.1 %attend.1 = bf16[128,512]{1,0:T(8,128)(2,1)} custom-call(bf16[128,4096]{1,0:T(8,128)(2,1)S(1)} %bitcast.22, bf16[128,512]{1,0:T(8,128)(2,1)S(1)} %bitcast.24, bf16[128,4096]{1,0:T(8,128)(2,1)S(1)} %bitcast.23, s32[1,128]{1,0:T(1,128)S(1)} %copy-done.16, s32[128,1]{1,0:T(8,128)S(1)} %copy.14.col_seg_ref), custom_call_target="tpu_custom_call" | custom-call | flops 268435456 | bytes 2097152 | tf_op jit(solution)/shard_map/attend/pallas_call | solution.py:94
  104.8 0.0 all-gather.6.cloned.1.call-update
  104.9 0.0 copy-done.13
  104.9 0.0 copy-start.4
  104.9 1.6 copy-done.4
  106.5 1.4 norm_forward.2
  107.8 22.4 %all-to-all-done.1.cot_ref = bf16[8,64,1024]{2,1,0:T(8,128)(2,1)} async-done(((bf16[8,64,1024]{2,1,0:T(8,128)(2,1)}), bf16[8,64,1024]{2,1,0:T(8,128)(2,1)}, u32[]{:S(2)}, u32[]{:S(2)}) %all-to-all-start.1) | async-done | bytes 1048608 | tf_op jit(solution)/shard_map/all_to_all | solution.py:216
  130.2 8.7 %all-to-all-start.2 = ((bf16[8,64,1024]{2,1,0:T(8,128)(2,1)}), bf16[8,64,1024]{2,1,0:T(8,128)(2,1)}, u32[]{:S(2)}, u32[]{:S(2)}) async-start(bf16[8,64,1024]{2,1,0:T(8,128)(2,1)} %norm_forward.2), calls=%async_computation.2 | async-start | bytes 2097152 | tf_op jit(solution)/shard_map/all_to_all | solution.py:216
  138.9 0.0 copy-done
  138.9 0.0 copy-done.14
  138.9 0.0 copy-start.1
  139.0 1.6 copy-done.1
  140.5 3.1 %norm_backward.3 = bf16[64,8192]{1,0:T(8,128)(2,1)} custom-call(bf16[8,64,1024]{2,1,0:T(8,128)(2,1)} %all-to-all-done.1.cot_ref, bf16[128,8192]{1,0:T(8,128)(2,1)S(1)} %bitcast.12, bf16[1,8192]{1,0:T(2,128)(2,1)S(1)} %copy-done.14, bf16[128,8192]{1,0:T(8,128)(2,1)S(1)} %bitcast.14), custom_call_target="tpu_custom_call" | custom-call | flops 5242880 | bytes 4194304 | tf_op jit(solution)/shard_map/norm_backward/pallas_call | solution.py:163
  143.7 2.4 %collective-permute-start.1 = (bf16[64,8192]{1,0:T(8,128)(2,1)}, bf16[64,8192]{1,0:T(8,128)(2,1)}, u32[]{:S(2)}, u32[]{:S(2)}) collective-permute-start(bf16[64,8192]{1,0:T(8,128)(2,1)} %norm_backward.3), channel_id=1, source_target_pairs={{8,0},{16,8},{24,16},{9,1},{17,9},{25,17},{10,2},{18,10},{26,18},{... | collective-permute-start | bytes 3145736 | tf_op jit(solution)/shard_map/ppermute | solution.py:23
  146.1 3.0 %norm_backward.2 = bf16[64,8192]{1,0:T(8,128)(2,1)} custom-call(bf16[8,64,1024]{2,1,0:T(8,128)(2,1)} %all-to-all-done.cot_ref, bf16[128,8192]{1,0:T(8,128)(2,1)S(1)} %bitcast.13, bf16[1,8192]{1,0:T(2,128)(2,1)S(1)} %copy-done.14, bf16[128,8192]{1,0:T(8,128)(2,1)S(1)} %bitcast.15), custom_call_target="tpu_custom_call" | custom-call | flops 5242880 | bytes 4194304 | tf_op jit(solution)/shard_map/norm_backward/pallas_call | solution.py:163
  149.1 1.9 collective-permute-start
  151.1 0.0 all-gather.6.cloned.1.call-done
  151.1 1.2 copy-done.8
  152.3 1.5 outer.2.rest_0_
  153.8 8.2 %all-to-all-done.2.columns_ref = bf16[8,64,1024]{2,1,0:T(8,128)(2,1)} async-done(((bf16[8,64,1024]{2,1,0:T(8,128)(2,1)}), bf16[8,64,1024]{2,1,0:T(8,128)(2,1)}, u32[]{:S(2)}, u32[]{:S(2)}) %all-to-all-start.2) | async-done | bytes 1048608 | tf_op jit(solution)/shard_map/all_to_all | solution.py:216
  162.1 1.2 copy-done.9
  163.3 4.1 %outer.3 = f32[1024,512]{1,0:T(8,128)} custom-call(bf16[8,64,1024]{2,1,0:T(8,128)(2,1)} %all-to-all-done.2.columns_ref, bf16[8,128,512]{2,1,0:T(8,128)(2,1)S(1)} %bitcast.21, f32[1024,512]{1,0:T(8,128)S(1)} %outer.2.rest_0_), custom_call_target="tpu_custom_call" | custom-call | flops 536870912 | bytes 2097152 | tf_op jit(solution)/shard_map/outer/pallas_call | solution.py:200
  167.4 5.4 %collective-permute-done.1 = bf16[64,8192]{1,0:T(8,128)(2,1)} collective-permute-done((bf16[64,8192]{1,0:T(8,128)(2,1)}, bf16[64,8192]{1,0:T(8,128)(2,1)}, u32[]{:S(2)}, u32[]{:S(2)}) %collective-permute-start.1) | collective-permute-done | bytes 1048608 | tf_op jit(solution)/shard_map/ppermute | solution.py:23
  172.8 21.7 %collective-permute-done = bf16[64,8192]{1,0:T(8,128)(2,1)} collective-permute-done((bf16[64,8192]{1,0:T(8,128)(2,1)}, bf16[64,8192]{1,0:T(8,128)(2,1)}, u32[]{:S(2)}, u32[]{:S(2)}) %collective-permute-start) | collective-permute-done | bytes 1048608 | tf_op jit(solution)/shard_map/ppermute | solution.py:23
  194.5 3.0 %maximum_bitcast_fusion = bf16[1,128,8192]{2,1,0:T(8,128)(2,1)} fusion(bf16[64,8192]{1,0:T(8,128)(2,1)} %collective-permute-done.1, bf16[64,8192]{1,0:T(8,128)(2,1)} %collective-permute-done), kind=kLoop, calls=%fused_computation | loop fusion | flops 4194304 | bytes 4194304 | tf_op jit(solution)/shard_map/broadcast_in_dim | solution.py:248
  (15 shorter events, 0.0 us)
Async XLA Ops:
  7.2 47.9 %all-gather.4.cloned.1.call-start = ((), (), s32[]{:S(2)}) async-start(), calls=%async_computation.4 | async-start | bytes 2359296 | tf_op jit(solution)/shard_map/all_gather | solution.py:234
  7.9 1.6 copy-start.3
  9.5 0.8 copy-start.12
  10.3 44.8 %copy-start.5 = (bf16[1,1024,1024]{2,1,0:T(8,128)(2,1)S(1)}, bf16[1,1024,1024]{2,1,0:T(8,128)(2,1)}, u32[]{:S(2)}) copy-start(bf16[1,1024,1024]{2,1,0:T(8,128)(2,1)} %param.21) | copy-start | bytes 6291460
  11.6 48.0 %all-to-all-start.3 = ((bf16[8,64,1024]{2,1,0:T(8,128)(2,1)}), bf16[8,64,1024]{2,1,0:T(8,128)(2,1)S(1)}, u32[]{:S(2)}, u32[]{:S(2)}) async-start(bf16[8,64,1024]{2,1,0:T(8,128)(2,1)} %norm_forward.3), calls=%async_computation.3 | async-start | bytes 2097152 | tf_op jit(solution)/shard_map/all_to_all | solution.py:216
  55.1 1.6 copy-start.6
  59.6 32.3 %all-to-all-start = ((bf16[8,64,1024]{2,1,0:T(8,128)(2,1)}), bf16[8,64,1024]{2,1,0:T(8,128)(2,1)}, u32[]{:S(2)}, u32[]{:S(2)}) async-start(bf16[8,64,1024]{2,1,0:T(8,128)(2,1)} %project.2), calls=%async_computation | async-start | bytes 2097152 | tf_op jit(solution)/shard_map/all_to_all | solution.py:216
  68.8 1.6 copy-start.7
  70.3 29.3 %copy-start.16 = (s32[1,128]{1,0:T(1,128)S(1)}, s32[1,128]{1,0:T(1,128)}, u32[]{:S(2)}) copy-start(s32[1,128]{1,0:T(1,128)} %row_seg_ref.1) | copy-start | bytes 1540
  70.3 29.4 %copy-start.15 = (bf16[1,128,512]{2,1,0:T(8,128)(2,1)S(1)}, bf16[1,128,512]{2,1,0:T(8,128)(2,1)}, u32[]{:S(2)}) copy-start(bf16[1,128,512]{2,1,0:T(8,128)(2,1)} %param.14) | copy-start | bytes 393220
  73.3 26.5 %copy-start.10 = (bf16[1,128,4096]{2,1,0:T(8,128)(2,1)S(1)}, bf16[1,128,4096]{2,1,0:T(8,128)(2,1)}, u32[]{:S(2)}) copy-start(bf16[1,128,4096]{2,1,0:T(8,128)(2,1)} %param.13) | copy-start | bytes 3145732
  73.3 26.5 %copy-start.11 = (bf16[1,128,4096]{2,1,0:T(8,128)(2,1)S(1)}, bf16[1,128,4096]{2,1,0:T(8,128)(2,1)}, u32[]{:S(2)}) copy-start(bf16[1,128,4096]{2,1,0:T(8,128)(2,1)} %param.15) | copy-start | bytes 3145732
  73.3 31.6 %copy-start.13 = (bf16[1,8192]{1,0:T(2,128)(2,1)S(1)}, bf16[1,8192]{1,0:T(2,128)(2,1)}, u32[]{:S(2)}) copy-start(bf16[1,8192]{1,0:T(2,128)(2,1)} %gain_ref.7) | copy-start | bytes 49156
  91.9 38.3 %all-to-all-start.1 = ((bf16[8,64,1024]{2,1,0:T(8,128)(2,1)}), bf16[8,64,1024]{2,1,0:T(8,128)(2,1)}, u32[]{:S(2)}, u32[]{:S(2)}) async-start(bf16[8,64,1024]{2,1,0:T(8,128)(2,1)} %project.3), calls=%async_computation.1 | async-start | bytes 2097152 | tf_op jit(solution)/shard_map/all_to_all | solution.py:216
  99.6 51.5 %all-gather.6.cloned.1.call-start = ((), (), s32[]{:S(2)}) async-start(), calls=%async_computation.5 | async-start | bytes 1179648 | tf_op jit(solution)/shard_map/all_gather | solution.py:237
  104.9 1.6 copy-start.4
  106.5 32.5 %copy-start = (bf16[1,128,8192]{2,1,0:T(8,128)(2,1)S(1)}, bf16[1,128,8192]{2,1,0:T(8,128)(2,1)}, u32[]{:S(2)}) copy-start(bf16[1,128,8192]{2,1,0:T(8,128)(2,1)} %param.17) | copy-start | bytes 6291460
  106.5 32.5 %copy-start.14 = (bf16[1,8192]{1,0:T(2,128)(2,1)S(1)}, bf16[1,8192]{1,0:T(2,128)(2,1)}, u32[]{:S(2)}) copy-start(bf16[1,8192]{1,0:T(2,128)(2,1)} %gain_ref.5) | copy-start | bytes 49156
  130.2 31.9 %all-to-all-start.2 = ((bf16[8,64,1024]{2,1,0:T(8,128)(2,1)}), bf16[8,64,1024]{2,1,0:T(8,128)(2,1)}, u32[]{:S(2)}, u32[]{:S(2)}) async-start(bf16[8,64,1024]{2,1,0:T(8,128)(2,1)} %norm_forward.2), calls=%async_computation.2 | async-start | bytes 2097152 | tf_op jit(solution)/shard_map/all_to_all | solution.py:216
  138.9 1.6 copy-start.1
  140.5 5.6 %copy-start.2 = (bf16[1,128,8192]{2,1,0:T(8,128)(2,1)S(1)}, bf16[1,128,8192]{2,1,0:T(8,128)(2,1)}, u32[]{:S(2)}) copy-start(bf16[1,128,8192]{2,1,0:T(8,128)(2,1)} %param.19) | copy-start | bytes 6291460
  143.7 29.1 %collective-permute-start.1 = (bf16[64,8192]{1,0:T(8,128)(2,1)}, bf16[64,8192]{1,0:T(8,128)(2,1)}, u32[]{:S(2)}, u32[]{:S(2)}) collective-permute-start(bf16[64,8192]{1,0:T(8,128)(2,1)} %norm_backward.3), channel_id=1, source_target_pairs={{8,0},{16,8},{24,16},{9,1},{17,9},{25,17},{10,2},{18,10},{26,18},{... | collective-permute-start | bytes 3145736 | tf_op jit(solution)/shard_map/ppermute | solution.py:23
  149.1 45.3 %collective-permute-start = (bf16[64,8192]{1,0:T(8,128)(2,1)}, bf16[64,8192]{1,0:T(8,128)(2,1)}, u32[]{:S(2)}, u32[]{:S(2)}) collective-permute-start(bf16[64,8192]{1,0:T(8,128)(2,1)} %norm_backward.2), channel_id=1, source_target_pairs={{8,0},{16,8},{24,16},{9,1},{17,9},{25,17},{10,2},{18,10},{26,18},{... | collective-permute-start | bytes 3145736 | tf_op jit(solution)/shard_map/ppermute | solution.py:23
  151.1 1.2 copy-start.8
  162.1 1.2 copy-start.9
Sparse Core Ops, SparseCore 0:
  9.6 45.4 all-gather.3
  105.0 30.0 all-gather.5
